TPU v7x, 512 devices: a whole 4x8x8 slice. The times are simulated.
512 devices in a mesh: vpair: 64 (over y_hi, z, x), occ: 8 (over y_lo, core).
Axes of the slice: x: 4, y: 8 (y_hi: 2, y_lo: 4; y = y_hi * 4 + y_lo), z: 8, core: 2. Of those that a mesh axis runs over, the one named last changes fastest.
Arguments:
- amplitudes: bfloat16 [64, 256, 128, 128], P('vpair', 'occ'), may hold values from -6 to 6
- fock_blocks: bfloat16 [8, 128, 128], replicated, may hold values from -0.5 to 0.5
- owner_map: int32 [64, 2], replicated, may hold values from 0 to 7, as said below
- extents: int32 [8], replicated, may hold values from 64 to 128
Outputs:
- doubles: bfloat16 [64, 256, 128, 128], P('vpair', 'occ')
Inputs may be any that keep to these rules, and one draw needn't show every extreme that they name: `owner_map`: rows s and s + 32 name mirrored blocks (A, B) and (B, A), or each names a diagonal pair (A, A); every ordered pair of blocks stands in exactly one row.
All inputs are finite; a program needn't handle non-finite values.
Results may differ from a plain program's by a relative error of at most 0.0079.
Values may be sent and summed in bfloat16 or wider, within the bound.
A program may use at most 64 MiB of HBM per device.

v0:
```python
import math

import jax
import jax.numpy as jnp
from jax import lax
from jax.sharding import PartitionSpec as P


def from_partner(value, axis, bit):
    mask = 2**bit
    pairs = [(source, source ^ mask) for source in range(lax.axis_size(axis))]
    return lax.ppermute(value, axis, pairs)


def body(amplitudes, fock_blocks, owner_map, extents):
    slots = amplitudes.shape[0]
    width = amplitudes.shape[2]
    nblocks = fock_blocks.shape[0]
    swap_bit = lax.axis_size("vpair").bit_length() - 2
    partner = from_partner(amplitudes, "vpair", swap_bit)
    first_slot = lax.axis_index("vpair") * slots
    labels = lax.dynamic_slice_in_dim(owner_map, first_slot, slots, 0)
    block_ids = jnp.arange(nblocks, dtype=jnp.int32)
    onehot_a = labels[:, 0:1] == block_ids[None, :]
    onehot_b = labels[:, 1:2] == block_ids[None, :]
    extent_a = jnp.sum(jnp.where(onehot_a, extents[None, :], 0), axis=1)
    extent_b = jnp.sum(jnp.where(onehot_b, extents[None, :], 0), axis=1)
    orbital = jnp.arange(width, dtype=jnp.int32)
    live = (orbital[None, :, None] < extent_a[:, None, None]) & (
        orbital[None, None, :] < extent_b[:, None, None]
    )
    diagonal_pair = labels[:, 0] == labels[:, 1]
    mirrored = jnp.where(diagonal_pair[:, None, None, None], amplitudes, partner)
    diff = amplitudes.astype(jnp.float32) - jnp.swapaxes(mirrored, 2, 3).astype(jnp.float32)
    anti = jnp.where(live[:, None], diff, jnp.float32(0.0)).astype(jnp.bfloat16)
    fock_a = jnp.einsum(
        "kn,nij->kij",
        onehot_a.astype(jnp.bfloat16),
        fock_blocks,
        preferred_element_type=jnp.float32,
    ).astype(jnp.bfloat16)
    fock_b = jnp.einsum(
        "kn,nij->kij",
        onehot_b.astype(jnp.bfloat16),
        fock_blocks,
        preferred_element_type=jnp.float32,
    ).astype(jnp.bfloat16)
    anti_rows = jnp.swapaxes(anti, 0, 1)
    local_rows = anti_rows.shape[0]

    def transform(tile_rows):
        half_image = jnp.einsum(
            "kji,qkjb->qkib", fock_a, tile_rows, preferred_element_type=jnp.float32
        ).astype(jnp.bfloat16)
        return jnp.einsum(
            "qkib,kbc->qkic", half_image, fock_b, preferred_element_type=jnp.float32
        ).astype(jnp.bfloat16)

    def contract(tile_rows):
        return jnp.einsum(
            "pkab,qkab->pq", anti_rows, transform(tile_rows), preferred_element_type=jnp.float32
        )

    all_rows = lax.all_gather(anti_rows, "occ", axis=0, tiled=True)
    nshards = all_rows.shape[0] // local_rows
    grouped = all_rows.reshape((nshards, local_rows) + anti_rows.shape[1:])
    columns = lax.map(contract, grouped)
    partial_sum = jnp.transpose(columns, (1, 0, 2)).reshape(local_rows, nshards * local_rows)
    summed = lax.psum(partial_sum, "vpair")
    intersection = (summed / float(nblocks * width)).astype(jnp.bfloat16)
    factor = 1.0 / math.sqrt(intersection.shape[1])
    result = jnp.einsum("pq,qkab->kpab", intersection, all_rows, preferred_element_type=jnp.float32)
    return (result * factor).astype(jnp.bfloat16)


def solution(mesh):
    placed = (P("vpair", "occ", None, None), P(), P(), P())
    return jax.shard_map(
        body, mesh=mesh, in_specs=placed, out_specs=P("vpair", "occ", None, None), check_vma=False
    )
```

profile of v0, /device:TPU:8, one launch (start us, length us, event | category | flops | bytes accessed | tf_op | source)
XLA Modules:
  0.0 656.5 jit_solution(7971819706587368980)
XLA Ops:
  6.6 2.0 copy.7
  8.6 6.8 %collective-permute-start = (bf16[1,32,128,128]{2,1,3,0:T(8,128)(2,1)S(1)}, bf16[1,32,128,128]{2,1,3,0:T(8,128)(2,1)S(1)}, u32[]{:S(2)}, u32[]{:S(2)}) collective-permute-start(bf16[1,32,128,128]{2,1,3,0:T(8,128)(2,1)S(1)} %copy.7), channel_id=1, source_target_pairs={{0,256},{8,264},{16,272},{24,280},{32,288},{40,296},{48,304},{56,3... | collective-permute-start | bytes 3145736 | tf_op jit(solution)/shard_map/ppermute | solution.py:12
  15.5 0.5 fusion.36
  17.3 1.9 fusion.31
  19.2 1.3 iota_compare_fusion
  20.6 41.2 %collective-permute-done = bf16[1,32,128,128]{2,1,3,0:T(8,128)(2,1)S(1)} collective-permute-done((bf16[1,32,128,128]{2,1,3,0:T(8,128)(2,1)S(1)}, bf16[1,32,128,128]{2,1,3,0:T(8,128)(2,1)S(1)}, u32[]{:S(2)}, u32[]{:S(2)}) %collective-permute-start) | collective-permute-done | bytes 1048608 | tf_op jit(solution)/shard_map/ppermute | solution.py:12
  61.8 2.0 fusion.12
  63.8 0.9 fusion.20
  64.7 0.8 fusion.18
  65.5 95.4 %all-gather.3.cloned.1.call-done = bf16[1,256,128,128]{3,1,2,0:T(8,128)(2,1)} async-done(((bf16[1,32,128,128]{3,1,2,0:T(8,128)(2,1)}), bf16[1,256,128,128]{3,1,2,0:T(8,128)(2,1)}) %all-gather.3.cloned.1.call-update) | async-done | bytes 8388624 | tf_op jit(solution)/shard_map/all_gather | solution.py:64
  160.9 41.1 %while.10 = (s32[]{:T(128)}, f32[8,32,32]{1,2,0:T(8,128)}, bf16[8,32,1,128,128]{4,1,0,3,2:T(8,128)(2,1)}, bf16[1,128,128]{2,1,0:T(8,128)(2,1)S(1)}, bf16[1,128,1...) while((s32[]{:T(128)}, f32[8,32,32]{1,2,0:T(8,128)}, ...), condition=%wide.region_3.4_spmd, body=%wide.region_2.3_spmd.sunk | while | flops 303038464 | bytes 14762605 | solution.py:67
  160.9 1.3 constant_dynamic-slice_fusion.3
  162.2 1.0 copy.24
  163.7 1.0 copy.25
  164.7 1.4 fusion.51
  166.1 1.3 constant_dynamic-slice_fusion.3
  167.4 1.0 copy.24
  168.8 1.0 copy.25
  169.8 1.4 fusion.51
  171.2 1.3 constant_dynamic-slice_fusion.3
  172.5 1.0 copy.24
  173.9 1.0 copy.25
  174.9 1.4 fusion.51
  176.3 1.3 constant_dynamic-slice_fusion.3
  177.6 1.0 copy.24
  178.7 0.4 fusion.50
  179.1 1.0 copy.25
  180.1 1.4 fusion.51
  181.5 1.3 constant_dynamic-slice_fusion.3
  182.8 1.0 copy.24
  184.2 1.0 copy.25
  185.2 1.4 fusion.51
  186.6 1.3 constant_dynamic-slice_fusion.3
  187.9 1.0 copy.24
  189.4 1.0 copy.25
  190.3 1.4 fusion.51
  191.7 1.3 constant_dynamic-slice_fusion.3
  193.1 1.0 copy.24
  194.5 1.0 copy.25
  195.5 1.4 fusion.51
  196.9 1.3 constant_dynamic-slice_fusion.3
  198.2 1.0 copy.24
  199.6 1.0 copy.25
  200.6 1.4 fusion.51
  202.0 1.0 copy.15
  203.0 440.3 %psum.7 = f32[32,256]{1,0:T(8,128)S(1)} all-reduce(f32[32,256]{1,0:T(8,128)S(1)} %copy.15), channel_id=1, replica_groups=mesh['vpair'=64,'occ'=8] {'vpair'}, use_global_device_ids=true, to_apply=%region_4.5 | all-reduce | flops 8192 | bytes 65536 | tf_op jit(solution)/shard_map/psum | solution.py:69
  643.3 4.9 fusion.15
  648.3 1.4 copy.10
  (37 shorter events, 3.2 us)
Async XLA Ops:
  6.5 57.2 %copy-start = (bf16[8,128,128]{2,1,0:T(8,128)(2,1)S(1)}, bf16[8,128,128]{2,1,0:T(8,128)(2,1)}, u32[]{:S(2)}) copy-start(bf16[8,128,128]{2,1,0:T(8,128)(2,1)} %param.7) | copy-start | bytes 786436
  6.5 55.2 %copy-start.2 = (bf16[1,32,128,128]{3,2,1,0:T(8,128)(2,1)S(1)}, bf16[1,32,128,128]{3,2,1,0:T(8,128)(2,1)}, u32[]{:S(2)}) copy-start(bf16[1,32,128,128]{3,2,1,0:T(8,128)(2,1)} %param.6) | copy-start | bytes 3145732
  6.5 8.9 %copy-start.3 = (s32[64,2]{0,1:T(2,128)S(1)}, s32[64,2]{0,1:T(2,128)}, u32[]{:S(2)}) copy-start(s32[64,2]{0,1:T(2,128)} %param.8) | copy-start | bytes 1540
  6.5 10.7 %copy-start.4 = (s32[8]{0:T(128)S(1)}, s32[8]{0:T(128)}, u32[]{:S(2)}) copy-start(s32[8]{0:T(128)} %param.9) | copy-start | bytes 100
  6.5 154.4 %all-gather.3.cloned.1.call-start = ((), (), s32[]{:S(2)}) async-start(), calls=%async_computation | async-start | bytes 9437184 | tf_op jit(solution)/shard_map/all_gather | solution.py:64
  8.6 53.2 %collective-permute-start = (bf16[1,32,128,128]{2,1,3,0:T(8,128)(2,1)S(1)}, bf16[1,32,128,128]{2,1,3,0:T(8,128)(2,1)S(1)}, u32[]{:S(2)}, u32[]{:S(2)}) collective-permute-start(bf16[1,32,128,128]{2,1,3,0:T(8,128)(2,1)S(1)} %copy.7), channel_id=1, source_target_pairs={{0,256},{8,264},{16,272},{24,280},{32,288},{40,296},{48,304},{56,3... | collective-permute-start | bytes 3145736 | tf_op jit(solution)/shard_map/ppermute | solution.py:12
  163.2 1.4 copy-start.1
  168.4 1.4 copy-start.1
  173.5 1.4 copy-start.1
  178.6 1.4 copy-start.1
  183.8 1.4 copy-start.1
  188.9 1.4 copy-start.1
  194.1 1.4 copy-start.1
  199.2 1.4 copy-start.1
Sparse Core Ops, SparseCore 0:
  63.9 96.9 all-gather.2
where the time goes:
time: 657 us; the launch traced here: 656 us
  blocking collectives  440 us (67%)
  waiting for transfers between devices  137 us (21%)
  local copies, waits for them, and re-layouts  31.2 us (5%)
  matrix products  21.2 us (3%)
  between operations  14.7 us (2%)
  starting transfers between devices  6.87 us (1%)
    psum x1, blocking collectives, body(): summed = lax.psum(partial_sum, 'vpair')  440 us
    all_gather x1, waiting for transfers between devices, body(): all_rows = lax.all_gather(anti_rows, 'occ', axis=0, tiled=True)  95.4 us
    ppermute x1, waiting for transfers between devices, from_partner(): return lax.ppermute(value, axis, pairs)  41.2 us
    dynamic_slice x16, local copies, waits for them, and re-layouts, body(): columns = lax.map(contract, grouped)  18.3 us
  transfers between devices with their start and end apart: 2, of which 2 were waited for; matrix products, arithmetic and copies ran while one was open for 1% of the time, Pallas kernels for 0%

commit v1 on v0

v1 whole, which is shorter than its diff:
```python
import functools
import math

import jax
import jax.numpy as jnp
from jax import lax
from jax.experimental import pallas as pl
from jax.experimental.pallas import tpu as pltpu
from jax.sharding import PartitionSpec as P

MESH = pl.DeviceIdType.MESH
CHUNKS = 4
NT = (((1,), (1,)), ((), ()))
NN = (((1,), (0,)), ((), ()))


def dot(left, right, dims):
    return lax.dot_general(left, right, dims, preferred_element_type=jnp.float32)


def kernel(
    sizes,
    amps, fock, owner, extents, out,
    own, received, fk, xf, yf, yb, tiles, acc, part_x, part_z, rows_own, rows_other, zs, packed_out,
    load_sem, ex_send, ex_recv, up_send, up_recv, down_send, down_recv,
    core_send, core_recv, x_send, x_recv, z_send, z_recv, swap_send, swap_recv, out_sem,
):
    ring, nz, nx = sizes
    half = ring // 2
    per_side = ring // 2
    plane = nz * nx
    mine, width = own.shape[0], own.shape[1]
    both = 2 * mine
    group = mine // CHUNKS
    span = width // CHUNKS

    v = lax.axis_index("vpair")
    o = lax.axis_index("occ")
    side = lax.div(v, plane)
    w = lax.rem(v, plane)
    z = lax.div(w, nx)
    x = lax.rem(w, nx)
    core = lax.rem(o, 2)
    y = side * per_side + lax.div(o, 2)

    def device(y_at, core_at, w_at):
        return (
            lax.div(y_at, per_side) * plane + w_at,
            lax.rem(y_at, per_side) * 2 + core_at,
        )

    mirror = device(lax.rem(y + half, ring), core, w)
    above = device(lax.rem(y + 1, ring), core, w)
    below = device(lax.rem(y + ring - 1, ring), core, w)
    sibling = device(y, 1 - core, w)
    x_at = [lax.rem(x + d, nx) for d in range(nx)]
    z_at = [lax.rem(z + d, nz) for d in range(nz)]
    x_peer = [device(y, core, z * nx + at) for at in x_at]
    z_peer = [device(y, core, at * nx + x) for at in z_at]

    loads = [
        pltpu.make_async_copy(
            amps.at[0, pl.ds(side * mine, mine)], own, load_sem.at[0]
        ),
        pltpu.make_async_copy(fock, fk, load_sem.at[1]),
    ]
    for copy in loads:
        copy.start()

    peers = [mirror, above, below, sibling] + x_peer[1:] + z_peer[1:]
    barrier = pltpu.get_barrier_semaphore()
    for peer in peers:
        pl.semaphore_signal(barrier, inc=1, device_id=peer, device_id_type=MESH)
    pl.semaphore_wait(barrier, len(peers))

    def remote(src, dst, send, recv, to):
        return pltpu.make_async_remote_copy(
            src_ref=src, dst_ref=dst, send_sem=send, recv_sem=recv,
            device_id=to, device_id_type=MESH,
        )

    def exchange(c):
        return remote(
            amps.at[0, pl.ds((1 - side) * mine + c * group, group)],
            received.at[pl.ds(c * group, group)],
            ex_send.at[c], ex_recv.at[c], mirror,
        )

    for c in range(CHUNKS):
        exchange(c).start()

    lower_slot = w
    upper_slot = w + plane
    a_low, b_low = owner[lower_slot, 0], owner[lower_slot, 1]
    a_high, b_high = owner[upper_slot, 0], owner[upper_slot, 1]
    off = (a_low != b_low).astype(jnp.int32)
    is_low = 1 - side
    row = lax.broadcasted_iota(jnp.int32, (width, width), 0)
    col = lax.broadcasted_iota(jnp.int32, (width, width), 1)
    above_diag = jnp.where(row < col, 1, 0)
    below_diag = jnp.where(row > col, 1, 0)
    first_i = jnp.minimum(above_diag + off, 1)
    second_i = below_diag * (1 - off)
    first = first_i > 0
    live = (row < jnp.where(first, extents[a_low], extents[a_high])) & (
        col < jnp.where(first, extents[b_low], extents[b_high])
    )
    plus_own = first_i == is_low
    minus_own = second_i == is_low

    for copy in loads:
        copy.wait()
    fock_a1, fock_b1 = fk[a_low], fk[b_low]
    fock_a2, fock_b2 = fk[a_high], fk[b_high]

    acc[...] = jnp.zeros_like(acc)

    def build(p, carry):
        mine_t = own[p].astype(jnp.float32)
        other_t = received[p].astype(jnp.float32)
        plus = jnp.where(plus_own, mine_t, other_t)
        minus = jnp.where(minus_own, mine_t, other_t)
        tile = jnp.where(live, plus - minus.T, 0.0).astype(jnp.bfloat16)
        tile = tile.astype(jnp.float32)
        turned = -tile.T
        one = jnp.where(first, tile, turned).astype(jnp.bfloat16)
        two = jnp.where(below_diag > 0, tile, turned).astype(jnp.bfloat16)
        half_one = dot(one, fock_b1, NT).astype(jnp.bfloat16)
        half_two = dot(two, fock_b2, NT).astype(jnp.bfloat16)
        image = jnp.where(
            first, dot(fock_a1, half_one, NN), dot(fock_a2, half_two, NN)
        )
        xf[pl.ds(p, width, stride=mine), :] = tile
        yf[pl.ds(p, width, stride=mine), :] = image
        return carry

    for c in range(CHUNKS):
        exchange(c).wait_recv()
        lax.fori_loop(c * group, (c + 1) * group, build, 0)

    def up(t, c):
        at = lax.rem(ring - t, ring) if not isinstance(t, int) else (ring - t) % ring
        return remote(
            tiles.at[at, 0, pl.ds(c * span, span)],
            tiles.at[ring - 1 - t, 0, pl.ds(c * span, span)],
            up_send.at[t, c], up_recv.at[t, c], above,
        )

    def down(t, c):
        return remote(
            tiles.at[t, 0, pl.ds(c * span, span)],
            tiles.at[t + 1, 0, pl.ds(c * span, span)],
            down_send.at[t, c], down_recv.at[t, c], below,
        )

    def across(r, c):
        return remote(
            tiles.at[r, 0, pl.ds(c * span, span)],
            tiles.at[r, 1, pl.ds(c * span, span)],
            core_send.at[r, c], core_recv.at[r, c], sibling,
        )

    for c in range(CHUNKS):
        block = xf[pl.ds(c * span * mine, span * mine), :].astype(jnp.bfloat16)
        tiles[0, 0, pl.ds(c * span, span)] = block.reshape(span, mine, width)
        up(0, c).start()
        down(0, c).start()
        across(0, c).start()
    for c in range(CHUNKS):
        block = yf[pl.ds(c * span * mine, span * mine), :].astype(jnp.bfloat16)
        yb[pl.ds(c * span, span)] = block.reshape(span, mine, width)

    unroll = min(8, span)

    def contract(slots, c):
        def some(i, sums):
            lefts, rights = [], []
            for u in range(unroll):
                a = c * span + i * unroll + u
                rights.append(yb[a])
                lefts.append(
                    jnp.concatenate([tiles[r, k, a] for r in slots for k in (0, 1)], 0)
                )
            return sums + dot(
                jnp.concatenate(lefts, 1), jnp.concatenate(rights, 1), NT
            )

        start = jnp.zeros((len(slots) * both, mine), jnp.float32)
        sums = lax.fori_loop(0, span // unroll, some, start)
        for n, r in enumerate(slots):
            acc[pl.ds(r * both, both), pl.ds(0, mine)] += sums[n * both : (n + 1) * both]

    def slots_at(t):
        return [t] if t in (0, half) else [t, ring - t]

    for t in range(half):
        for c in range(CHUNKS):
            up_here = t < half - 1 or c < CHUNKS // 2
            down_here = t < half - 1 or c >= CHUNKS // 2
            if up_here:
                up(t, c).wait_recv()
                if t + 1 < half - 1 or (t + 1 == half - 1 and c < CHUNKS // 2):
                    up(t + 1, c).start()
                across(ring - 1 - t, c).start()
            if down_here:
                down(t, c).wait_recv()
                if t + 1 < half - 1 or (t + 1 == half - 1 and c >= CHUNKS // 2):
                    down(t + 1, c).start()
                across(t + 1, c).start()
            for r in slots_at(t):
                across(r, c).wait_recv()
            contract(slots_at(t), c)
    for c in range(CHUNKS):
        across(half, c).wait_recv()
        contract([half], c)

    rows = ring * both
    turned = jnp.concatenate(
        [acc[pl.ds(n * width, width), :].T[:mine] for n in range(rows // width)], 1
    )
    part_x[x] = turned
    def send_x(d):
        return remote(part_x.at[x], part_x.at[x], x_send.at[d], x_recv.at[x], x_peer[d])

    def wait_x(d):
        return remote(
            part_x.at[x_at[d]], part_x.at[x_at[d]], x_send.at[d], x_recv.at[x_at[d]], x_peer[d]
        )

    def send_z(d):
        return remote(part_z.at[z], part_z.at[z], z_send.at[d], z_recv.at[z], z_peer[d])

    def wait_z(d):
        return remote(
            part_z.at[z_at[d]], part_z.at[z_at[d]], z_send.at[d], z_recv.at[z_at[d]], z_peer[d]
        )

    for d in range(1, nx):
        send_x(d).start()
    for d in range(1, nx):
        wait_x(d).wait_recv()
    total = part_x[0]
    for n in range(1, nx):
        total += part_x[n]
    part_z[z] = total
    for d in range(1, nz):
        send_z(d).start()
    for d in range(1, nz):
        wait_z(d).wait_recv()
    total = part_z[0]
    for n in range(1, nz):
        total += part_z[n]

    nblocks = fk.shape[0]
    rows_own[...] = (total * (2.0 / (nblocks * width))).astype(jnp.bfloat16)
    swap = remote(rows_own, rows_other, swap_send.at[0], swap_recv.at[0], mirror)
    swap.start()
    swap.wait_recv()
    here = rows_own[...].astype(jnp.float32)
    there = rows_other[...].astype(jnp.float32)
    cut = half * both
    there = jnp.concatenate([there[:, cut:], there[:, :cut]], 1)
    low = jnp.zeros(here.shape, jnp.int32) + side == 0
    inter = jnp.concatenate(
        [jnp.where(low, here, there), jnp.where(low, there, here)], 0
    ).astype(jnp.bfloat16)
    factor = 1.0 / math.sqrt(rows)

    pair = 2

    def residual(i, carry):
        a = i * pair
        right = jnp.concatenate(
            [tiles[:, :, a + u].reshape(rows, width) for u in range(pair)], 1
        )
        made = dot(inter, right, NN) * factor
        for u in range(pair):
            zs[pl.ds((a + u) * both, both), :] = made[:, u * width : (u + 1) * width]
        return carry

    lax.fori_loop(0, width // pair, residual, 0)

    triangle = is_low * above_diag + side * below_diag
    keep = (off * is_low + (1 - off) * triangle) > 0

    def unpack(p, carry):
        tile = zs[pl.ds(p, width, stride=both), :]
        packed_out[p] = jnp.where(keep, tile, -tile.T).astype(jnp.bfloat16)
        return carry

    def write(c):
        size = both // CHUNKS
        return pltpu.make_async_copy(
            packed_out.at[pl.ds(c * size, size)], out.at[0, pl.ds(c * size, size)], out_sem.at[c]
        )

    for c in range(CHUNKS):
        size = both // CHUNKS
        lax.fori_loop(c * size, (c + 1) * size, unpack, 0)
        write(c).start()

    for c in range(CHUNKS):
        exchange(c).wait_send()
        for t in range(half):
            if t < half - 1 or c < CHUNKS // 2:
                up(t, c).wait_send()
            if t < half - 1 or c >= CHUNKS // 2:
                down(t, c).wait_send()
        for r in range(ring):
            across(r, c).wait_send()
    for d in range(1, nx):
        send_x(d).wait_send()
    for d in range(1, nz):
        send_z(d).wait_send()
    swap.wait_send()
    for c in range(CHUNKS):
        write(c).wait()


def body(sizes, amplitudes, fock_blocks, owner_map, extents):
    ring, nz, nx = sizes
    slots, both, width = amplitudes.shape[0], amplitudes.shape[1], amplitudes.shape[2]
    mine = both // 2
    half = ring // 2
    rows = ring * both
    dma = pltpu.SemaphoreType.DMA
    any_space = pl.BlockSpec(memory_space=pl.ANY)
    smem = pl.BlockSpec(memory_space=pltpu.SMEM)
    bf16, f32 = jnp.bfloat16, jnp.float32
    return pl.pallas_call(
        functools.partial(kernel, sizes),
        out_shape=jax.ShapeDtypeStruct((slots, both, width, width), bf16),
        in_specs=[any_space, any_space, smem, smem],
        out_specs=any_space,
        scratch_shapes=[
            pltpu.VMEM((mine, width, width), bf16),
            pltpu.VMEM((mine, width, width), bf16),
            pltpu.VMEM(fock_blocks.shape, bf16),
            pltpu.VMEM((width * mine, width), f32),
            pltpu.VMEM((width * mine, width), f32),
            pltpu.VMEM((width, mine, width), bf16),
            pltpu.VMEM((ring, 2, width, mine, width), bf16),
            pltpu.VMEM((rows, width), f32),
            pltpu.VMEM((nx, mine, rows), f32),
            pltpu.VMEM((nz, mine, rows), f32),
            pltpu.VMEM((mine, rows), bf16),
            pltpu.VMEM((mine, rows), bf16),
            pltpu.VMEM((width * both, width), f32),
            pltpu.VMEM((both, width, width), bf16),
            dma((2,)),
            dma((CHUNKS,)), dma((CHUNKS,)),
            dma((half, CHUNKS)), dma((half, CHUNKS)),
            dma((half, CHUNKS)), dma((half, CHUNKS)),
            dma((ring, CHUNKS)), dma((ring, CHUNKS)),
            dma((nx,)), dma((nx,)),
            dma((nz,)), dma((nz,)),
            dma((1,)), dma((1,)),
            dma((CHUNKS,)),
        ],
        compiler_params=pltpu.CompilerParams(
            collective_id=0, has_side_effects=True, vmem_limit_bytes=48 * 1024 * 1024
        ),
        cost_estimate=pl.CostEstimate(
            flops=2**30, bytes_accessed=2**22, transcendentals=0
        ),
    )(amplitudes, fock_blocks, owner_map, extents)


def solution(mesh):
    plane = mesh.shape["vpair"] // 2
    nx = 4 if plane % 4 == 0 else 1
    sizes = (mesh.shape["occ"], plane // nx, nx)
    placed = (P("vpair", "occ", None, None), P(), P(), P())
    return jax.shard_map(
        functools.partial(body, sizes),
        mesh=mesh,
        in_specs=placed,
        out_specs=P("vpair", "occ", None, None),
        check_vma=False,
    )
```

time: 657 us -> 121 us (0.18)
  blocking collectives: 440 us -> 0 us
  waiting for transfers between devices: 137 us -> 0 us
  Pallas kernels: 0 us -> 117 us
  local copies, waits for them, and re-layouts: 31.2 us -> 3.93 us
  matrix products: 21.2 us -> 0 us
  between operations: 14.7 us -> 0.02 us
  starting transfers between devices: 6.87 us -> 0 us
    psum x1 -> x0, blocking collectives: 440 us -> none  [body(): summed = lax.psum(partial_sum, 'vpair')]
    pallas_call x0 -> x1, Pallas kernels: none -> 117 us  [body(): pl.pallas_call(functools.partial(kernel, sizes), out_shape=jax.ShapeDtype...]
    all_gather x1 -> x0, waiting for transfers between devices: 95.4 us -> none  [body(): all_rows = lax.all_gather(anti_rows, 'occ', axis=0, tiled=True)]
    ppermute x1 -> x0, waiting for transfers between devices: 41.2 us -> none  [from_partner(): return lax.ppermute(value, axis, pairs)]
    dot_general x19 -> x0, matrix products: 21.2 us -> none  [the longest x8 11.2 us: contract(): jnp.einsum('pkab,qkab->pq', anti_rows, transform(tile_rows), preferred_el...]
    dynamic_slice x17 -> x0, local copies, waits for them, and re-layouts: 18.4 us -> none  [the longest x16 18.3 us: body(): columns = lax.map(contract, grouped)]
    another operation x8 -> x0, local copies, waits for them, and re-layouts: 7.8 us -> none
    ppermute x1 -> x0, starting transfers between devices: 6.83 us -> none  [from_partner(): return lax.ppermute(value, axis, pairs)]
  transfers between devices with their start and end apart: 2 -> 0, of which waited for: 2 -> 0; matrix products, arithmetic and copies ran while one was open for 1% -> 0% of each run, Pallas kernels for 0% -> 0%
where the time goes in v1:
time: 121 us
  Pallas kernels  117 us (97%)
  local copies, waits for them, and re-layouts  3.93 us (3%)
    pallas_call x1, Pallas kernels, body(): pl.pallas_call(functools.partial(kernel, sizes), out_shape=jax.ShapeDtype...  117 us
    unnamed x8, local copies, waits for them, and re-layouts  3.93 us

profile of v1, /device:TPU:8, one launch (start us, length us, event | category | flops | bytes accessed | tf_op | source)
XLA Modules:
  0.0 120.8 jit_solution(4634255020252750976)
XLA Ops:
  0.0 0.0 copy-start.2
  0.0 0.8 copy.5.owner
  0.8 0.0 copy-done.2
  0.8 0.0 copy-start
  0.8 1.2 %copy-done = bf16[1,32,128,128]{3,2,1,0:T(8,128)(2,1)S(1)} copy-done((bf16[1,32,128,128]{3,2,1,0:T(8,128)(2,1)S(1)}, bf16[1,32,128,128]{3,2,1,0:T(8,128)(2,1)}, u32[]{:S(2)}) %copy-start) | copy-done | bytes 1048600
  2.0 0.0 copy-start.1
  2.0 0.9 copy-done.1
  3.0 116.8 %shard_map.46 = bf16[1,32,128,128]{3,2,1,0:T(8,128)(2,1)S(1)} custom-call(bf16[1,32,128,128]{3,2,1,0:T(8,128)(2,1)S(1)} %copy-done, bf16[8,128,128]{2,1,0:T(8,128)(2,1)S(1)} %copy-done.1, s32[64,2]{1,0:T(8,128)S(1)} %copy.5.owner, s32[8]{0:T(128)S(1)} %copy-done.2), custom_call_target="tpu_custom_call" | custom-call | flops 1073741824 | bytes 4194304 | tf_op jit(solution)/shard_map/pallas_call | solution.py:330
  119.8 1.0 copy.7
Async XLA Ops:
  0.0 0.8 copy-start.2
  0.8 1.2 %copy-start = (bf16[1,32,128,128]{3,2,1,0:T(8,128)(2,1)S(1)}, bf16[1,32,128,128]{3,2,1,0:T(8,128)(2,1)}, u32[]{:S(2)}) copy-start(bf16[1,32,128,128]{3,2,1,0:T(8,128)(2,1)} %amps.1) | copy-start | bytes 3145732
  2.0 0.9 copy-start.1

commit v2 on v1

v2 whole, which is shorter than its diff:
```python
import functools
import math

import jax
import jax.numpy as jnp
from jax import lax
from jax.experimental import pallas as pl
from jax.experimental.pallas import tpu as pltpu
from jax.sharding import PartitionSpec as P

MESH = pl.DeviceIdType.MESH
CHUNKS = 4
DEPTH = 4
NT = (((1,), (1,)), ((), ()))
NN = (((1,), (0,)), ((), ()))


def dot(left, right, dims):
    return lax.dot_general(left, right, dims, preferred_element_type=jnp.float32)


def kernel(
    sizes,
    amps, fock, owner_at, extents_at, out,
    owner, extents, own, received, fk, xf, yf, yb, tiles, acc, part_x, part_z, row_parts, zs,
    load_sem, ex_send, ex_recv, up_send, up_recv, down_send, down_recv,
    core_send, core_recv, x_send, x_recv, z_send, z_recv, row_send, row_recv,
):
    ring, nz, nx = sizes
    half = ring // 2
    per_side = ring // 2
    plane = nz * nx
    mine, width = own.shape[0], own.shape[1]
    both = 2 * mine
    group = mine // CHUNKS
    span = width // CHUNKS

    v = lax.axis_index("vpair")
    o = lax.axis_index("occ")
    side = lax.div(v, plane)
    w = lax.rem(v, plane)
    z = lax.div(w, nx)
    x = lax.rem(w, nx)
    core = lax.rem(o, 2)
    y = side * per_side + lax.div(o, 2)

    def device(y_at, core_at, w_at):
        return (
            lax.div(y_at, per_side) * plane + w_at,
            lax.rem(y_at, per_side) * 2 + core_at,
        )

    around = [device(lax.rem(y + d, ring), core, w) for d in range(ring)]
    mirror, above, below = around[half], around[1], around[ring - 1]
    sibling = device(y, 1 - core, w)
    x_at = [lax.rem(x + d, nx) for d in range(nx)]
    z_at = [lax.rem(z + d, nz) for d in range(nz)]
    x_peer = [device(y, core, z * nx + at) for at in x_at]
    z_peer = [device(y, core, at * nx + x) for at in z_at]

    loads = [
        pltpu.make_async_copy(
            amps.at[0, pl.ds(side * mine, mine)], own, load_sem.at[0]
        ),
        pltpu.make_async_copy(fock, fk, load_sem.at[1]),
        pltpu.make_async_copy(owner_at, owner, load_sem.at[2]),
        pltpu.make_async_copy(extents_at, extents, load_sem.at[3]),
    ]
    for copy in loads:
        copy.start()

    peers = around[1:] + [sibling] + x_peer[1:] + z_peer[1:]
    barrier = pltpu.get_barrier_semaphore()
    for peer in peers:
        pl.semaphore_signal(barrier, inc=1, device_id=peer, device_id_type=MESH)
    pl.semaphore_wait(barrier, len(peers))

    def remote(src, dst, send, recv, to):
        return pltpu.make_async_remote_copy(
            src_ref=src, dst_ref=dst, send_sem=send, recv_sem=recv,
            device_id=to, device_id_type=MESH,
        )

    def exchange(c):
        return remote(
            amps.at[0, pl.ds((1 - side) * mine + c * group, group)],
            received.at[pl.ds(c * group, group)],
            ex_send.at[c], ex_recv.at[c], mirror,
        )

    for c in range(CHUNKS):
        exchange(c).start()

    for copy in loads:
        copy.wait()

    lower_slot = w
    upper_slot = w + plane
    a_low, b_low = owner[0, lower_slot], owner[1, lower_slot]
    a_high, b_high = owner[0, upper_slot], owner[1, upper_slot]
    off = (a_low != b_low).astype(jnp.int32)
    is_low = 1 - side
    row = lax.broadcasted_iota(jnp.int32, (width, width), 0)
    col = lax.broadcasted_iota(jnp.int32, (width, width), 1)
    above_diag = jnp.where(row < col, 1, 0)
    below_diag = jnp.where(row > col, 1, 0)
    first_i = jnp.minimum(above_diag + off, 1)
    second_i = below_diag * (1 - off)
    first = first_i > 0
    live = (row < jnp.where(first, extents[a_low], extents[a_high])) & (
        col < jnp.where(first, extents[b_low], extents[b_high])
    )
    plus_own = first_i == is_low
    minus_own = second_i == is_low

    fock_a1, fock_b1 = fk[a_low], fk[b_low]
    fock_a2, fock_b2 = fk[a_high], fk[b_high]

    acc[...] = jnp.zeros_like(acc)

    def transform_tile(p, tile):
        turned = -tile.T
        one = jnp.where(first, tile, turned).astype(jnp.bfloat16)
        two = jnp.where(below_diag > 0, tile, turned).astype(jnp.bfloat16)
        half_one = dot(one, fock_b1, NT).astype(jnp.bfloat16)
        half_two = dot(two, fock_b2, NT).astype(jnp.bfloat16)
        yf[pl.ds(p, width, stride=mine), :] = jnp.where(
            first, dot(fock_a1, half_one, NN), dot(fock_a2, half_two, NN)
        )

    def build(p, carry):
        mine_t = own[p].astype(jnp.float32)
        other_t = received[p].astype(jnp.float32)
        plus = jnp.where(plus_own, mine_t, other_t)
        minus = jnp.where(minus_own, mine_t, other_t)
        tile = jnp.where(live, plus - minus.T, 0.0).astype(jnp.bfloat16)
        tile = tile.astype(jnp.float32)
        xf[pl.ds(p, width, stride=mine), :] = tile
        transform_tile(p, tile)
        return carry

    def transform(p, carry):
        transform_tile(p, xf[pl.ds(p, width, stride=mine), :])
        return carry

    for c in range(CHUNKS):
        exchange(c).wait_recv()
        lax.fori_loop(c * group, (c + 1) * group, build, 0, unroll=4)

    def up(t, c):
        at = lax.rem(ring - t, ring) if not isinstance(t, int) else (ring - t) % ring
        return remote(
            tiles.at[at, 0, pl.ds(c * span, span)],
            tiles.at[ring - 1 - t, 0, pl.ds(c * span, span)],
            up_send.at[t, c], up_recv.at[t, c], above,
        )

    def down(t, c):
        return remote(
            tiles.at[t, 0, pl.ds(c * span, span)],
            tiles.at[t + 1, 0, pl.ds(c * span, span)],
            down_send.at[t, c], down_recv.at[t, c], below,
        )

    def across(r, c):
        return remote(
            tiles.at[r, 0, pl.ds(c * span, span)],
            tiles.at[r, 1, pl.ds(c * span, span)],
            core_send.at[r, c], core_recv.at[r, c], sibling,
        )

    middle = CHUNKS // 2
    up_order = list(range(CHUNKS))
    down_order = up_order[middle:] + up_order[:middle]
    up_steps = [(t, c) for t in range(half) for c in up_order][: -middle]
    down_steps = [(t, c) for t in range(half) for c in down_order][: -middle]

    def start(i):
        if i < len(up_steps):
            up(*up_steps[i]).start()
            down(*down_steps[i]).start()

    def own_chunk(c):
        block = xf[pl.ds(c * span * mine, span * mine), :].astype(jnp.bfloat16)
        tiles[0, 0, pl.ds(c * span, span)] = block.reshape(span, mine, width)

    for i in range(CHUNKS):
        if i < middle:
            own_chunk(up_order[i])
            own_chunk(down_order[i])
        start(i)
    for c in range(CHUNKS):
        across(0, c).start()

    def image_done(n):
        def some(c, carry):
            block = yf[pl.ds(c * span * mine, span * mine), :].astype(jnp.bfloat16)
            yb[n, pl.ds(c * span, span)] = block.reshape(span, mine, width)
            return carry

        lax.fori_loop(0, CHUNKS, some, 0)

    def block_in(r):
        def some(c, carry):
            block = tiles[r, 0, pl.ds(c * span, span)].reshape(span * mine, width)
            xf[pl.ds(c * span * mine, span * mine), :] = block.astype(jnp.float32)
            return carry

        lax.fori_loop(0, CHUNKS, some, 0)

    image_done(0)
    unroll = min(32, span)

    def contract(n, slots, to, begin, count):
        def some(i, sums):
            lefts, rights = [], []
            for u in range(unroll):
                a = begin + i * unroll + u
                rights.append(yb[n, a])
                lefts.append(
                    jnp.concatenate([tiles[r, k, a] for r in slots for k in (0, 1)], 0)
                )
            return sums + dot(
                jnp.concatenate(lefts, 1), jnp.concatenate(rights, 1), NT
            )

        zero = jnp.zeros((len(slots) * both, mine), jnp.float32)
        sums = lax.fori_loop(0, count // unroll, some, zero, unroll=min(4, count // unroll))
        for m, r in enumerate(to):
            acc[pl.ds(r * both, both), pl.ds(0, mine)] += sums[m * both : (m + 1) * both]

    def receive(i):
        t, c = up_steps[i]
        up(t, c).wait_recv()
        up(t, c).wait_send()
        across(ring - 1 - t, c).start()
        t, c = down_steps[i]
        down(t, c).wait_recv()
        down(t, c).wait_send()
        across(t + 1, c).start()
        start(i + DEPTH)

    def arrived(r, c):
        across(r, c).wait_recv()

    def send_x(d):
        return remote(part_x.at[x], part_x.at[x], x_send.at[d], x_recv.at[x], x_peer[d])

    def wait_x(d):
        return remote(
            part_x.at[x_at[d]], part_x.at[x_at[d]], x_send.at[d], x_recv.at[x_at[d]], x_peer[d]
        )

    def send_z(d):
        return remote(part_z.at[z], part_z.at[z], z_send.at[d], z_recv.at[z], z_peer[d])

    def wait_z(d):
        return remote(
            part_z.at[z_at[d]], part_z.at[z_at[d]], z_send.at[d], z_recv.at[z_at[d]], z_peer[d]
        )

    def send_rows(d):
        return remote(
            row_parts[0], row_parts[ring - d], row_send.at[d], row_recv.at[ring - d], around[d]
        )

    for i in range(CHUNKS):
        receive(i)
        arrived(0, i)
        contract(0, [0], [0], i * span, span)
    for i in range(CHUNKS):
        receive(CHUNKS + i)
        for r in (1, ring - 1):
            arrived(r, i)
        contract(0, [1, ring - 1], [1, ring - 1], i * span, span)
        block, part = i // 2, i % 2
        if part == 0:
            block_in((ring - 1, 1)[block])
        lax.fori_loop(part * (mine // 2), (part + 1) * (mine // 2), transform, 0, unroll=8)
        if part == 1:
            image_done(1 + block)

    for c in range(CHUNKS):
        arrived(2, c)
        arrived(ring - 2, c)
    contract(0, [2, ring - 2], [2, ring - 2], 0, width)
    contract(1, [2], [3], 0, width)
    contract(2, [ring - 2], [ring - 3], 0, width)
    block_in(ring - 2)
    lax.fori_loop(0, mine, transform, 0, unroll=8)
    image_done(3)
    contract(3, [2], [4], 0, width)

    rows = ring * both
    part_x[x] = jnp.concatenate(
        [acc[pl.ds(n * width, width), :].T[:mine] for n in range(rows // width)], 1
    )
    for d in range(1, nx):
        send_x(d).start()
    receive(2 * CHUNKS)
    receive(2 * CHUNKS + 1)
    for d in range(1, nx):
        wait_x(d).wait_recv()
    total = part_x[0]
    for n in range(1, nx):
        total += part_x[n]
    part_z[z] = total
    for d in range(1, nz):
        send_z(d).start()
    receive(2 * CHUNKS + 2)
    for d in range(1, nz):
        wait_z(d).wait_recv()
    total = part_z[0]
    for n in range(1, nz):
        total += part_z[n]
    nblocks = fk.shape[0]
    row_parts[0][...] = (total * (2.0 / (nblocks * width))).astype(jnp.bfloat16)
    for d in range(1, ring):
        send_rows(d).start()
    receive(2 * CHUNKS + 3)
    for d in range(1, ring):
        send_rows(ring - d).wait_recv()

    place = lax.div(lax.broadcasted_iota(jnp.int32, (mine, rows), 1), both)

    def rows_of(d):
        near, after, before, far = [
            row_parts[(d + n) % ring][...].astype(jnp.float32) for n in (0, 1, ring - 1, 2)
        ]
        return jnp.where(
            place == 3, after, jnp.where(place == ring - 3, before, jnp.where(place == 4, far, near))
        )

    here, there = rows_of(0), rows_of(half)
    cut = half * both
    there = jnp.concatenate([there[:, cut:], there[:, :cut]], 1)
    low = jnp.zeros(here.shape, jnp.int32) + side == 0
    inter = jnp.concatenate(
        [jnp.where(low, here, there), jnp.where(low, there, here)], 0
    ).astype(jnp.bfloat16)
    factor = 1.0 / math.sqrt(rows)
    pair = 2

    def residual(i, carry):
        a = i * pair
        right = jnp.concatenate(
            [tiles[:, :, a + u].reshape(rows, width) for u in range(pair)], 1
        )
        made = dot(inter, right, NN) * factor
        for u in range(pair):
            zs[pl.ds((a + u) * both, both), :] = made[:, u * width : (u + 1) * width]
        return carry

    for i in range(middle):
        receive((half - 1) * CHUNKS + i)
        for c in (up_order[i], down_order[i]):
            for r in range(3, ring - 2):
                arrived(r, c)
            lax.fori_loop(c * span // pair, (c + 1) * span // pair, residual, 0, unroll=8)

    triangle = is_low * above_diag + side * below_diag
    keep = (off * is_low + (1 - off) * triangle) > 0

    def unpack(p, carry):
        tile = zs[pl.ds(p, width, stride=both), :]
        out[0, p] = jnp.where(keep, tile, -tile.T).astype(jnp.bfloat16)
        return carry

    lax.fori_loop(0, both, unpack, 0, unroll=4)

    for c in range(CHUNKS):
        exchange(c).wait_send()
        for r in range(ring):
            across(r, c).wait_send()
    for d in range(1, nx):
        send_x(d).wait_send()
    for d in range(1, nz):
        send_z(d).wait_send()
    for d in range(1, ring):
        send_rows(d).wait_send()


def body(sizes, amplitudes, fock_blocks, owner_map, extents):
    ring, nz, nx = sizes
    slots, both, width = amplitudes.shape[0], amplitudes.shape[1], amplitudes.shape[2]
    mine = both // 2
    half = ring // 2
    rows = ring * both
    dma = pltpu.SemaphoreType.DMA
    hbm = pl.BlockSpec(memory_space=pltpu.HBM)
    bf16, f32 = jnp.bfloat16, jnp.float32
    return pl.pallas_call(
        functools.partial(kernel, sizes),
        out_shape=jax.ShapeDtypeStruct((slots, both, width, width), bf16),
        in_specs=[hbm, hbm, hbm, hbm],
        out_specs=pl.BlockSpec(memory_space=pltpu.VMEM),
        scratch_shapes=[
            pltpu.SMEM(owner_map.shape[::-1], jnp.int32),
            pltpu.SMEM(extents.shape, jnp.int32),
            pltpu.VMEM((mine, width, width), bf16),
            pltpu.VMEM((mine, width, width), bf16),
            pltpu.VMEM(fock_blocks.shape, bf16),
            pltpu.VMEM((width * mine, width), f32),
            pltpu.VMEM((width * mine, width), f32),
            pltpu.VMEM((4, width, mine, width), bf16),
            pltpu.VMEM((ring, 2, width, mine, width), bf16),
            pltpu.VMEM((rows, width), f32),
            pltpu.VMEM((nx, mine, rows), f32),
            pltpu.VMEM((nz, mine, rows), f32),
            [pltpu.VMEM((mine, rows), bf16)] * ring,
            pltpu.VMEM((width * both, width), f32),
            dma((4,)),
            dma((CHUNKS,)), dma((CHUNKS,)),
            dma((half, CHUNKS)), dma((half, CHUNKS)),
            dma((half, CHUNKS)), dma((half, CHUNKS)),
            dma((ring, CHUNKS)), dma((ring, CHUNKS)),
            dma((nx,)), dma((nx,)),
            dma((nz,)), dma((nz,)),
            dma((ring,)), dma((ring,)),
        ],
        compiler_params=pltpu.CompilerParams(
            collective_id=0, has_side_effects=True, vmem_limit_bytes=63 * 1024 * 1024
        ),
        cost_estimate=pl.CostEstimate(
            flops=2**30, bytes_accessed=2**22, transcendentals=0
        ),
    )(amplitudes, fock_blocks, owner_map.T, extents)


def solution(mesh):
    plane = mesh.shape["vpair"] // 2
    nx = 4 if plane % 4 == 0 else 1
    sizes = (mesh.shape["occ"], plane // nx, nx)
    placed = (P("vpair", "occ", None, None), P(), P(), P())
    return jax.shard_map(
        functools.partial(body, sizes),
        mesh=mesh,
        in_specs=placed,
        out_specs=P("vpair", "occ", None, None),
        check_vma=False,
    )
```

time: 121 us -> 98.9 us (0.82)
  the two profiles are of different devices: /device:TPU:8 before, /device:TPU:1 now
where the time goes in v2:
time: 98.9 us; the launch traced here: 98.8 us
  Pallas kernels  96.4 us (97%)
  local copies, waits for them, and re-layouts  2.31 us (2%)
    pallas_call x1, Pallas kernels, body(): pl.pallas_call(functools.partial(kernel, sizes), out_shape=jax.ShapeDtype...  96.4 us
    unnamed x1, local copies, waits for them, and re-layouts  2.31 us

profile of v2, /device:TPU:1, one launch (start us, length us, event | category | flops | bytes accessed | tf_op | source)
XLA Modules:
  0.0 98.8 jit_solution(11327799778635311288)
XLA Ops:
  0.0 96.4 %shard_map.46 = bf16[1,32,128,128]{3,2,1,0:T(8,128)(2,1)} custom-call(bf16[1,32,128,128]{3,2,1,0:T(8,128)(2,1)} %amps.1, bf16[8,128,128]{2,1,0:T(8,128)(2,1)} %fock.1, s32[2,64]{1,0:T(2,128)} %bitcast.1, s32[8]{0:T(128)} %extents_at.1), custom_call_target="tpu_custom_call" | custom-call | flops 1073741824 | bytes 4194304 | tf_op jit(solution)/shard_map/pallas_call | solution.py:392
  96.5 2.3 %copy.6 = bf16[1,32,128,128]{3,2,1,0:T(8,128)(2,1)} copy(bf16[1,32,128,128]{3,2,1,0:T(8,128)(2,1)} %shard_map.46) | data formatting | bytes 2097152

commit v3 on v2

--- a/solution.py
+++ b/solution.py
@@ -22,7 +22,7 @@
 def kernel(
     sizes,
     amps, fock, owner_at, extents_at, out,
-    owner, extents, own, received, fk, xf, yf, yb, tiles, acc, part_x, part_z, row_parts, zs,
+    owner, extents, own, received, fk, xf, yf, hf, yb, tiles, acc, part_x, part_z, row_parts, zs,
     load_sem, ex_send, ex_recv, up_send, up_recv, down_send, down_recv,
     core_send, core_recv, x_send, x_recv, z_send, z_recv, row_send, row_recv,
 ):
@@ -118,29 +118,12 @@
 
     acc[...] = jnp.zeros_like(acc)
 
-    def transform_tile(p, tile):
-        turned = -tile.T
-        one = jnp.where(first, tile, turned).astype(jnp.bfloat16)
-        two = jnp.where(below_diag > 0, tile, turned).astype(jnp.bfloat16)
-        half_one = dot(one, fock_b1, NT).astype(jnp.bfloat16)
-        half_two = dot(two, fock_b2, NT).astype(jnp.bfloat16)
-        yf[pl.ds(p, width, stride=mine), :] = jnp.where(
-            first, dot(fock_a1, half_one, NN), dot(fock_a2, half_two, NN)
-        )
-
     def build(p, carry):
         mine_t = own[p].astype(jnp.float32)
         other_t = received[p].astype(jnp.float32)
         plus = jnp.where(plus_own, mine_t, other_t)
         minus = jnp.where(minus_own, mine_t, other_t)
-        tile = jnp.where(live, plus - minus.T, 0.0).astype(jnp.bfloat16)
-        tile = tile.astype(jnp.float32)
-        xf[pl.ds(p, width, stride=mine), :] = tile
-        transform_tile(p, tile)
-        return carry
-
-    def transform(p, carry):
-        transform_tile(p, xf[pl.ds(p, width, stride=mine), :])
+        xf[pl.ds(p, width, stride=mine), :] = jnp.where(live, plus - minus.T, 0.0)
         return carry
 
     for c in range(CHUNKS):
@@ -188,35 +171,49 @@
         if i < middle:
             own_chunk(up_order[i])
             own_chunk(down_order[i])
-        start(i)
+        if i < DEPTH:
+            start(i)
     for c in range(CHUNKS):
         across(0, c).start()
 
-    def image_done(n):
-        def some(c, carry):
+    def right_factor(n, r, c):
+        block = tiles[r, 0, pl.ds(c * span, span)].reshape(span * mine, width)
+        block = block.astype(jnp.float32)
+        at_a = lax.div(lax.broadcasted_iota(jnp.int32, block.shape, 0), mine) + c * span
+        at_b = lax.broadcasted_iota(jnp.int32, block.shape, 1)
+        upper = jnp.where(at_a < at_b, 1, 0) + off > 0
+        for m, (keep_here, factor_b) in enumerate(((upper, fock_b1), (at_a > at_b, fock_b2))):
+            part = jnp.where(keep_here, block, 0.0).astype(jnp.bfloat16)
+            made = dot(part, factor_b, NT).astype(jnp.bfloat16)
+            hf[n, m, pl.ds(c * span * mine, span * mine), :] = made.astype(jnp.float32)
+
+    def left_factor(n, to):
+        def some(p, carry):
+            one = hf[n, 0, pl.ds(p, width, stride=mine), :].astype(jnp.bfloat16)
+            two = hf[n, 1, pl.ds(p, width, stride=mine), :].astype(jnp.bfloat16)
+            one, two = dot(fock_a1, one, NN), dot(fock_a2, two, NN)
+            turned = jnp.where(below_diag > 0, one, two).T
+            yf[pl.ds(p, width, stride=mine), :] = jnp.where(first, one, two) - jnp.where(
+                off > 0, 0.0, turned
+            )
+            return carry
+
+        def narrow(c, carry):
             block = yf[pl.ds(c * span * mine, span * mine), :].astype(jnp.bfloat16)
-            yb[n, pl.ds(c * span, span)] = block.reshape(span, mine, width)
+            yb[to, pl.ds(c * span, span)] = block.reshape(span, mine, width)
             return carry
 
-        lax.fori_loop(0, CHUNKS, some, 0)
-
-    def block_in(r):
-        def some(c, carry):
-            block = tiles[r, 0, pl.ds(c * span, span)].reshape(span * mine, width)
-            xf[pl.ds(c * span * mine, span * mine), :] = block.astype(jnp.float32)
-            return carry
-
-        lax.fori_loop(0, CHUNKS, some, 0)
-
-    image_done(0)
+        lax.fori_loop(0, mine, some, 0, unroll=mine)
+        lax.fori_loop(0, CHUNKS, narrow, 0)
+
     unroll = min(32, span)
 
-    def contract(n, slots, to, begin, count):
+    def contract(images, slots, to, begin, count):
         def some(i, sums):
             lefts, rights = [], []
             for u in range(unroll):
                 a = begin + i * unroll + u
-                rights.append(yb[n, a])
+                rights.append(jnp.concatenate([yb[n, a] for n in images], 0))
                 lefts.append(
                     jnp.concatenate([tiles[r, k, a] for r in slots for k in (0, 1)], 0)
                 )
@@ -224,10 +221,12 @@
                 jnp.concatenate(lefts, 1), jnp.concatenate(rights, 1), NT
             )
 
-        zero = jnp.zeros((len(slots) * both, mine), jnp.float32)
-        sums = lax.fori_loop(0, count // unroll, some, zero, unroll=min(4, count // unroll))
-        for m, r in enumerate(to):
-            acc[pl.ds(r * both, both), pl.ds(0, mine)] += sums[m * both : (m + 1) * both]
+        zero = jnp.zeros((len(slots) * both, len(images) * mine), jnp.float32)
+        sums = lax.fori_loop(0, count // unroll, some, zero, unroll=count // unroll)
+        for m in range(len(slots)):
+            for n in range(len(images)):
+                made = sums[m * both : (m + 1) * both, n * mine : (n + 1) * mine]
+                acc[pl.ds(to[m][n] * both, both), pl.ds(0, mine)] += made
 
     def receive(i):
         t, c = up_steps[i]
@@ -264,32 +263,44 @@
             row_parts[0], row_parts[ring - d], row_send.at[d], row_recv.at[ring - d], around[d]
         )
 
+    last = ring - 1
+    for c in range(CHUNKS):
+        right_factor(0, 0, c)
+    left_factor(0, 0)
     for i in range(CHUNKS):
         receive(i)
+        right_factor(0, last, up_order[i])
+        right_factor(1, 1, down_order[i])
         arrived(0, i)
-        contract(0, [0], [0], i * span, span)
+        if i == middle:
+            contract([0], [0], [[0]], 0, width // 2)
+    contract([0], [0], [[0]], width // 2, width // 2)
+
+    halves = (0, width // 2)
     for i in range(CHUNKS):
         receive(CHUNKS + i)
-        for r in (1, ring - 1):
-            arrived(r, i)
-        contract(0, [1, ring - 1], [1, ring - 1], i * span, span)
-        block, part = i // 2, i % 2
-        if part == 0:
-            block_in((ring - 1, 1)[block])
-        lax.fori_loop(part * (mine // 2), (part + 1) * (mine // 2), transform, 0, unroll=8)
-        if part == 1:
-            image_done(1 + block)
-
-    for c in range(CHUNKS):
-        arrived(2, c)
-        arrived(ring - 2, c)
-    contract(0, [2, ring - 2], [2, ring - 2], 0, width)
-    contract(1, [2], [3], 0, width)
-    contract(2, [ring - 2], [ring - 3], 0, width)
-    block_in(ring - 2)
-    lax.fori_loop(0, mine, transform, 0, unroll=8)
-    image_done(3)
-    contract(3, [2], [4], 0, width)
+        right_factor(2, last - 1, up_order[i])
+        if i == 0:
+            for c in range(CHUNKS):
+                arrived(1, c)
+                arrived(last, c)
+        if i < 2:
+            left_factor(i, 1 + i)
+        if i == 1:
+            contract([0], [1, last], [[1], [last]], 0, width)
+        if i == 2:
+            for j in range(middle):
+                arrived(2, down_order[j])
+                arrived(last - 1, up_order[j])
+            contract([0, 1], [2], [[2, 3]], halves[1], width // 2)
+            contract([0, 2], [last - 1], [[last - 1, last - 2]], halves[0], width // 2)
+    left_factor(2, 3)
+    for j in range(middle, CHUNKS):
+        arrived(2, down_order[j])
+        arrived(last - 1, up_order[j])
+    contract([0, 1], [2], [[2, 3]], halves[0], width // 2)
+    contract([0, 2], [last - 1], [[last - 1, last - 2]], halves[1], width // 2)
+    contract([3], [2], [[4]], 0, width)
 
     rows = ring * both
     part_x[x] = jnp.concatenate(
@@ -356,7 +367,7 @@
         for c in (up_order[i], down_order[i]):
             for r in range(3, ring - 2):
                 arrived(r, c)
-            lax.fori_loop(c * span // pair, (c + 1) * span // pair, residual, 0, unroll=8)
+            lax.fori_loop(c * span // pair, (c + 1) * span // pair, residual, 0, unroll=16)
 
     triangle = is_low * above_diag + side * below_diag
     keep = (off * is_low + (1 - off) * triangle) > 0
@@ -366,7 +377,7 @@
         out[0, p] = jnp.where(keep, tile, -tile.T).astype(jnp.bfloat16)
         return carry
 
-    lax.fori_loop(0, both, unpack, 0, unroll=4)
+    lax.fori_loop(0, both, unpack, 0, unroll=8)
 
     for c in range(CHUNKS):
         exchange(c).wait_send()
@@ -402,6 +413,7 @@
             pltpu.VMEM(fock_blocks.shape, bf16),
             pltpu.VMEM((width * mine, width), f32),
             pltpu.VMEM((width * mine, width), f32),
+            pltpu.VMEM((3, 2, width * mine, width), f32),
             pltpu.VMEM((4, width, mine, width), bf16),
             pltpu.VMEM((ring, 2, width, mine, width), bf16),
             pltpu.VMEM((rows, width), f32),
@@ -419,12 +431,15 @@
             dma((ring,)), dma((ring,)),
         ],
         compiler_params=pltpu.CompilerParams(
-            collective_id=0, has_side_effects=True, vmem_limit_bytes=63 * 1024 * 1024
+            collective_id=0, has_side_effects=True, vmem_limit_bytes=48 * 1024 * 1024
         ),
         cost_estimate=pl.CostEstimate(
             flops=2**30, bytes_accessed=2**22, transcendentals=0
         ),
-    )(amplitudes, fock_blocks, owner_map.T, extents)
+    )(*[
+        pltpu.with_memory_space_constraint(value, pltpu.HBM)
+        for value in (amplitudes, fock_blocks, owner_map.T, extents)
+    ])
 
 
 def solution(mesh):

time: 98.9 us -> 90.5 us (0.915)
  Pallas kernels: 96.4 us -> 89.4 us
  local copies, waits for them, and re-layouts: 2.31 us -> 0.97 us
    pallas_call x1, Pallas kernels: 96.4 us -> 89.4 us  [body(): pl.pallas_call(functools.partial(kernel, sizes), out_shape=jax.ShapeDtype...]
    unnamed x1, local copies, waits for them, and re-layouts: 2.31 us -> 0.97 us
where the time goes in v3:
time: 90.5 us; the launch traced here: 90.4 us
  Pallas kernels  89.4 us (99%)
  local copies, waits for them, and re-layouts  0.97 us (1%)
    pallas_call x1, Pallas kernels, body(): pl.pallas_call(functools.partial(kernel, sizes), out_shape=jax.ShapeDtype...  89.4 us

profile of v3, /device:TPU:1, one launch (start us, length us, event | category | flops | bytes accessed | tf_op | source)
XLA Modules:
  0.0 90.4 jit_solution(994707889440137372)
XLA Ops:
  0.0 89.4 %shard_map.46 = bf16[1,32,128,128]{3,2,1,0:T(8,128)(2,1)S(1)} custom-call(bf16[1,32,128,128]{3,2,1,0:T(8,128)(2,1)} %amps.1, bf16[8,128,128]{2,1,0:T(8,128)(2,1)} %fock.1, s32[2,64]{1,0:T(2,128)} %bitcast.1, s32[8]{0:T(128)} %extents_at.1), custom_call_target="tpu_custom_call" | custom-call | flops 1073741824 | bytes 4194304 | tf_op jit(solution)/shard_map/pallas_call | solution.py:403
  89.4 1.0 %copy.6 = bf16[1,32,128,128]{3,2,1,0:T(8,128)(2,1)} copy(bf16[1,32,128,128]{3,2,1,0:T(8,128)(2,1)S(1)} %shard_map.46) | data formatting | bytes 2097152

commit v4 on v3

--- a/solution.py
+++ b/solution.py
@@ -10,7 +10,6 @@
 
 MESH = pl.DeviceIdType.MESH
 CHUNKS = 4
-DEPTH = 4
 NT = (((1,), (1,)), ((), ()))
 NN = (((1,), (0,)), ((), ()))
 
@@ -22,15 +21,15 @@
 def kernel(
     sizes,
     amps, fock, owner_at, extents_at, out,
-    owner, extents, own, received, fk, xf, yf, hf, yb, tiles, acc, part_x, part_z, row_parts, zs,
-    load_sem, ex_send, ex_recv, up_send, up_recv, down_send, down_recv,
-    core_send, core_recv, x_send, x_recv, z_send, z_recv, row_send, row_recv,
+    owner, extents, from_below, from_above, fk, xf, yf, hf, yb, tiles, acc, part_x, part_z, row_left, row_right, zs,
+    load_sem, ex_up_send, ex_up_recv, ex_down_send, ex_down_recv, up_send, up_recv, down_send, down_recv,
+    core_send, core_recv, x_send, x_recv, z_send, z_recv, left_send, left_recv, right_send, right_recv,
 ):
     ring, nz, nx = sizes
     half = ring // 2
     per_side = ring // 2
     plane = nz * nx
-    mine, width = own.shape[0], own.shape[1]
+    mine, width = from_below.shape[0], from_below.shape[1]
     both = 2 * mine
     group = mine // CHUNKS
     span = width // CHUNKS
@@ -51,7 +50,7 @@
         )
 
     around = [device(lax.rem(y + d, ring), core, w) for d in range(ring)]
-    mirror, above, below = around[half], around[1], around[ring - 1]
+    above, below = around[1], around[ring - 1]
     sibling = device(y, 1 - core, w)
     x_at = [lax.rem(x + d, nx) for d in range(nx)]
     z_at = [lax.rem(z + d, nz) for d in range(nz)]
@@ -59,12 +58,9 @@
     z_peer = [device(y, core, at * nx + x) for at in z_at]
 
     loads = [
-        pltpu.make_async_copy(
-            amps.at[0, pl.ds(side * mine, mine)], own, load_sem.at[0]
-        ),
         pltpu.make_async_copy(fock, fk, load_sem.at[1]),
         pltpu.make_async_copy(owner_at, owner, load_sem.at[2]),
-        pltpu.make_async_copy(extents_at, extents, load_sem.at[3]),
+        pltpu.make_async_copy(extents_at, extents, load_sem.at[0]),
     ]
     for copy in loads:
         copy.start()
@@ -81,15 +77,25 @@
             device_id=to, device_id_type=MESH,
         )
 
-    def exchange(c):
+    reach = half // 2
+
+    def exchange_up(c):
+        return remote(
+            amps.at[0, pl.ds(side * mine + c * group, group)],
+            from_below.at[pl.ds(c * group, group)],
+            ex_up_send.at[c], ex_up_recv.at[c], around[reach],
+        )
+
+    def exchange_down(c):
         return remote(
             amps.at[0, pl.ds((1 - side) * mine + c * group, group)],
-            received.at[pl.ds(c * group, group)],
-            ex_send.at[c], ex_recv.at[c], mirror,
+            from_above.at[pl.ds(c * group, group)],
+            ex_down_send.at[c], ex_down_recv.at[c], around[ring - reach],
         )
 
     for c in range(CHUNKS):
-        exchange(c).start()
+        exchange_up(c).start()
+        exchange_down(c).start()
 
     for copy in loads:
         copy.wait()
@@ -100,6 +106,8 @@
     a_high, b_high = owner[0, upper_slot], owner[1, upper_slot]
     off = (a_low != b_low).astype(jnp.int32)
     is_low = 1 - side
+    below_is_low = lax.div(lax.rem(y + ring - reach, ring), half) == 0
+    below_is_low = below_is_low.astype(jnp.int32)
     row = lax.broadcasted_iota(jnp.int32, (width, width), 0)
     col = lax.broadcasted_iota(jnp.int32, (width, width), 1)
     above_diag = jnp.where(row < col, 1, 0)
@@ -110,8 +118,8 @@
     live = (row < jnp.where(first, extents[a_low], extents[a_high])) & (
         col < jnp.where(first, extents[b_low], extents[b_high])
     )
-    plus_own = first_i == is_low
-    minus_own = second_i == is_low
+    plus_below = first_i == below_is_low
+    minus_below = second_i == below_is_low
 
     fock_a1, fock_b1 = fk[a_low], fk[b_low]
     fock_a2, fock_b2 = fk[a_high], fk[b_high]
@@ -119,15 +127,16 @@
     acc[...] = jnp.zeros_like(acc)
 
     def build(p, carry):
-        mine_t = own[p].astype(jnp.float32)
-        other_t = received[p].astype(jnp.float32)
-        plus = jnp.where(plus_own, mine_t, other_t)
-        minus = jnp.where(minus_own, mine_t, other_t)
+        one = from_below[p].astype(jnp.float32)
+        two = from_above[p].astype(jnp.float32)
+        plus = jnp.where(plus_below, one, two)
+        minus = jnp.where(minus_below, one, two)
         xf[pl.ds(p, width, stride=mine), :] = jnp.where(live, plus - minus.T, 0.0)
         return carry
 
     for c in range(CHUNKS):
-        exchange(c).wait_recv()
+        exchange_up(c).wait_recv()
+        exchange_down(c).wait_recv()
         lax.fori_loop(c * group, (c + 1) * group, build, 0, unroll=4)
 
     def up(t, c):
@@ -158,11 +167,6 @@
     up_steps = [(t, c) for t in range(half) for c in up_order][: -middle]
     down_steps = [(t, c) for t in range(half) for c in down_order][: -middle]
 
-    def start(i):
-        if i < len(up_steps):
-            up(*up_steps[i]).start()
-            down(*down_steps[i]).start()
-
     def own_chunk(c):
         block = xf[pl.ds(c * span * mine, span * mine), :].astype(jnp.bfloat16)
         tiles[0, 0, pl.ds(c * span, span)] = block.reshape(span, mine, width)
@@ -171,8 +175,8 @@
         if i < middle:
             own_chunk(up_order[i])
             own_chunk(down_order[i])
-        if i < DEPTH:
-            start(i)
+        up(*up_steps[i]).start()
+        down(*down_steps[i]).start()
     for c in range(CHUNKS):
         across(0, c).start()
 
@@ -231,13 +235,14 @@
     def receive(i):
         t, c = up_steps[i]
         up(t, c).wait_recv()
-        up(t, c).wait_send()
+        if i + CHUNKS < len(up_steps):
+            up(*up_steps[i + CHUNKS]).start()
         across(ring - 1 - t, c).start()
         t, c = down_steps[i]
         down(t, c).wait_recv()
-        down(t, c).wait_send()
+        if i + CHUNKS < len(down_steps):
+            down(*down_steps[i + CHUNKS]).start()
         across(t + 1, c).start()
-        start(i + DEPTH)
 
     def arrived(r, c):
         across(r, c).wait_recv()
@@ -258,10 +263,21 @@
             part_z.at[z_at[d]], part_z.at[z_at[d]], z_send.at[d], z_recv.at[z_at[d]], z_peer[d]
         )
 
-    def send_rows(d):
-        return remote(
-            row_parts[0], row_parts[ring - d], row_send.at[d], row_recv.at[ring - d], around[d]
-        )
+    left_to = (1, 2, ring - 3, ring - 2)
+    right_to = (2, 3, half, ring - 2, ring - 1)
+
+    def send_left(d):
+        return remote(
+            row_left[0], row_left[ring - d], left_send.at[d], left_recv.at[ring - d], around[d]
+        )
+
+    def send_right(d):
+        return remote(
+            row_right[0], row_right[ring - d], right_send.at[d], right_recv.at[ring - d], around[d]
+        )
+
+    def row_sends():
+        return [send_left(d) for d in left_to] + [send_right(d) for d in right_to]
 
     last = ring - 1
     for c in range(CHUNKS):
@@ -325,26 +341,37 @@
     for n in range(1, nz):
         total += part_z[n]
     nblocks = fk.shape[0]
-    row_parts[0][...] = (total * (2.0 / (nblocks * width))).astype(jnp.bfloat16)
-    for d in range(1, ring):
-        send_rows(d).start()
+    made = (total * (2.0 / (nblocks * width))).astype(jnp.bfloat16)
+    row_left[0][...] = made[:, : rows // 2]
+    row_right[0][...] = made[:, rows // 2 :]
+    for copy in row_sends():
+        copy.start()
     receive(2 * CHUNKS + 3)
-    for d in range(1, ring):
-        send_rows(ring - d).wait_recv()
-
-    place = lax.div(lax.broadcasted_iota(jnp.int32, (mine, rows), 1), both)
+    receive(3 * CHUNKS)
+    receive(3 * CHUNKS + 1)
+    for copy in row_sends():
+        copy.wait_recv()
+
+    place = lax.div(lax.broadcasted_iota(jnp.int32, (mine, rows // 2), 1), both)
 
     def rows_of(d):
-        near, after, before, far = [
-            row_parts[(d + n) % ring][...].astype(jnp.float32) for n in (0, 1, ring - 1, 2)
-        ]
-        return jnp.where(
-            place == 3, after, jnp.where(place == ring - 3, before, jnp.where(place == 4, far, near))
-        )
-
-    here, there = rows_of(0), rows_of(half)
-    cut = half * both
-    there = jnp.concatenate([there[:, cut:], there[:, :cut]], 1)
+        left = jnp.where(
+            place == 3,
+            row_left[(d + 1) % ring][...].astype(jnp.float32),
+            row_left[d][...].astype(jnp.float32),
+        )
+        right = jnp.where(
+            place == 0,
+            row_right[(d + 2) % ring][...].astype(jnp.float32),
+            jnp.where(
+                place == 1,
+                row_right[d - 1][...].astype(jnp.float32),
+                row_right[d][...].astype(jnp.float32),
+            ),
+        )
+        return pltpu.roll(jnp.concatenate([left, right], 1), d * both, 1)
+
+    here, there = rows_of(reach), rows_of(ring - reach)
     low = jnp.zeros(here.shape, jnp.int32) + side == 0
     inter = jnp.concatenate(
         [jnp.where(low, here, there), jnp.where(low, there, here)], 0
@@ -363,7 +390,6 @@
         return carry
 
     for i in range(middle):
-        receive((half - 1) * CHUNKS + i)
         for c in (up_order[i], down_order[i]):
             for r in range(3, ring - 2):
                 arrived(r, c)
@@ -380,15 +406,19 @@
     lax.fori_loop(0, both, unpack, 0, unroll=8)
 
     for c in range(CHUNKS):
-        exchange(c).wait_send()
+        exchange_up(c).wait_send()
+        exchange_down(c).wait_send()
         for r in range(ring):
             across(r, c).wait_send()
+    for i in range(len(up_steps)):
+        up(*up_steps[i]).wait_send()
+        down(*down_steps[i]).wait_send()
     for d in range(1, nx):
         send_x(d).wait_send()
     for d in range(1, nz):
         send_z(d).wait_send()
-    for d in range(1, ring):
-        send_rows(d).wait_send()
+    for copy in row_sends():
+        copy.wait_send()
 
 
 def body(sizes, amplitudes, fock_blocks, owner_map, extents):
@@ -419,16 +449,17 @@
             pltpu.VMEM((rows, width), f32),
             pltpu.VMEM((nx, mine, rows), f32),
             pltpu.VMEM((nz, mine, rows), f32),
-            [pltpu.VMEM((mine, rows), bf16)] * ring,
+            [pltpu.VMEM((mine, rows // 2), bf16)] * ring,
+            [pltpu.VMEM((mine, rows // 2), bf16)] * ring,
             pltpu.VMEM((width * both, width), f32),
-            dma((4,)),
-            dma((CHUNKS,)), dma((CHUNKS,)),
+            dma((3,)),
+            dma((CHUNKS,)), dma((CHUNKS,)), dma((CHUNKS,)), dma((CHUNKS,)),
             dma((half, CHUNKS)), dma((half, CHUNKS)),
             dma((half, CHUNKS)), dma((half, CHUNKS)),
             dma((ring, CHUNKS)), dma((ring, CHUNKS)),
             dma((nx,)), dma((nx,)),
             dma((nz,)), dma((nz,)),
-            dma((ring,)), dma((ring,)),
+            dma((ring,)), dma((ring,)), dma((ring,)), dma((ring,)),
         ],
         compiler_params=pltpu.CompilerParams(
             collective_id=0, has_side_effects=True, vmem_limit_bytes=48 * 1024 * 1024

time: 90.5 us -> 86.9 us (0.960)
  the two profiles are of different devices: /device:TPU:1 before, /device:TPU:8 now
where the time goes in v4:
time: 86.9 us; the launch traced here: 86.8 us
  Pallas kernels  85.9 us (99%)
  local copies, waits for them, and re-layouts  0.97 us (1%)
    pallas_call x1, Pallas kernels, body(): pl.pallas_call(functools.partial(kernel, sizes), out_shape=jax.ShapeDtype...  85.9 us

profile of v4, /device:TPU:8, one launch (start us, length us, event | category | flops | bytes accessed | tf_op | source)
XLA Modules:
  0.0 86.8 jit_solution(16176239209881131479)
XLA Ops:
  0.0 85.9 %shard_map.46 = bf16[1,32,128,128]{3,2,1,0:T(8,128)(2,1)S(1)} custom-call(bf16[1,32,128,128]{3,2,1,0:T(8,128)(2,1)} %amps.1, bf16[8,128,128]{2,1,0:T(8,128)(2,1)} %fock.1, s32[2,64]{1,0:T(2,128)} %bitcast.1, s32[8]{0:T(128)} %extents_at.1), custom_call_target="tpu_custom_call" | custom-call | flops 1073741824 | bytes 4194304 | tf_op jit(solution)/shard_map/pallas_call | solution.py:433
  85.9 1.0 %copy.6 = bf16[1,32,128,128]{3,2,1,0:T(8,128)(2,1)} copy(bf16[1,32,128,128]{3,2,1,0:T(8,128)(2,1)S(1)} %shard_map.46) | data formatting | bytes 2097152

commit v5 on v4

--- a/solution.py
+++ b/solution.py
@@ -441,9 +441,9 @@
             pltpu.VMEM((mine, width, width), bf16),
             pltpu.VMEM((mine, width, width), bf16),
             pltpu.VMEM(fock_blocks.shape, bf16),
-            pltpu.VMEM((width * mine, width), f32),
-            pltpu.VMEM((width * mine, width), f32),
-            pltpu.VMEM((3, 2, width * mine, width), f32),
+            pltpu.VMEM((width * mine + mine, width), f32),
+            pltpu.VMEM((width * mine + mine, width), f32),
+            pltpu.VMEM((3, 2, width * mine + mine, width), f32),
             pltpu.VMEM((4, width, mine, width), bf16),
             pltpu.VMEM((ring, 2, width, mine, width), bf16),
             pltpu.VMEM((rows, width), f32),
@@ -451,7 +451,7 @@
             pltpu.VMEM((nz, mine, rows), f32),
             [pltpu.VMEM((mine, rows // 2), bf16)] * ring,
             [pltpu.VMEM((mine, rows // 2), bf16)] * ring,
-            pltpu.VMEM((width * both, width), f32),
+            pltpu.VMEM((width * both + both, width), f32),
             dma((3,)),
             dma((CHUNKS,)), dma((CHUNKS,)), dma((CHUNKS,)), dma((CHUNKS,)),
             dma((half, CHUNKS)), dma((half, CHUNKS)),

time: 86.9 us -> 86.9 us (level)
  no operation moved by 1% of the time
where the time goes in v5:
time: 86.9 us; the launch traced here: 86.8 us
  Pallas kernels  85.9 us (99%)
  local copies, waits for them, and re-layouts  0.97 us (1%)
    pallas_call x1, Pallas kernels, body(): pl.pallas_call(functools.partial(kernel, sizes), out_shape=jax.ShapeDtype...  85.9 us

profile of v5, /device:TPU:8, one launch (start us, length us, event | category | flops | bytes accessed | tf_op | source)
XLA Modules:
  0.0 86.8 jit_solution(983577721050989850)
XLA Ops:
  0.0 85.9 %shard_map.46 = bf16[1,32,128,128]{3,2,1,0:T(8,128)(2,1)S(1)} custom-call(bf16[1,32,128,128]{3,2,1,0:T(8,128)(2,1)} %amps.1, bf16[8,128,128]{2,1,0:T(8,128)(2,1)} %fock.1, s32[2,64]{1,0:T(2,128)} %bitcast.1, s32[8]{0:T(128)} %extents_at.1), custom_call_target="tpu_custom_call" | custom-call | flops 1073741824 | bytes 4194304 | tf_op jit(solution)/shard_map/pallas_call | solution.py:433
  85.9 1.0 %copy.6 = bf16[1,32,128,128]{3,2,1,0:T(8,128)(2,1)} copy(bf16[1,32,128,128]{3,2,1,0:T(8,128)(2,1)S(1)} %shard_map.46) | data formatting | bytes 2097152
